TPU v7x, 512 devices: a whole 4x8x8 slice. The times are simulated.
512 devices in a mesh: deg: 64 (over y, z_lo, core), row: 8 (over x, z_hi).
Axes of the slice: x: 4, y: 8, z: 8 (z_hi: 2, z_lo: 4; z = z_hi * 4 + z_lo), core: 2. Of those that a mesh axis runs over, the one named last changes fastest.
Arguments:
- left_factor: float32 [16384, 16, 64], P('deg', 'row'), may hold values from 0 to 7340032, as said below
- right_factor: float32 [16384, 64, 64], P('deg', 'row'), may hold values from 0 to 7340032, as said below
Outputs:
- product_coeffs: float32 [32768, 16, 64], P('deg', 'row')
Inputs may be any that keep to these rules, and one draw needn't show every extreme that they name: `left_factor`: whole numbers, each a residue modulo the prime 7340033; both ends occur. `right_factor`: whole numbers, each a residue modulo the prime 7340033; both ends occur.
All inputs are finite; a program needn't handle non-finite values.
Results may differ from a plain program's by a relative error of at most 0.0003.
Values sent between devices are 32-bit elements; how exact they have to be, the bound alone decides.
A program may use at most 128 MiB of HBM per device.

v0:
```python
import numpy as np
import jax
import jax.numpy as jnp
from jax import lax
from jax.experimental import pallas as pl
from jax.experimental.pallas import tpu as pltpu
from jax.sharding import PartitionSpec as P

modulus = 7340033
generator = 3
inverse_modulus = 1.0 / modulus
modulus_high = float(modulus - 1)

BLOCK = 256
POINTS = 2 * BLOCK
KD = 64
CD = 64


def powers(root, exponents, order):
    table = np.ones(order, np.int64)
    for position in range(1, order):
        table[position] = table[position - 1] * root % modulus
    return table[exponents % order]


def digit_rows(values):
    centred = np.where(values > modulus // 2, values - modulus, values)
    digits = []
    for _ in range(2):
        low = (centred + 128) % 256 - 128
        digits.append(low)
        centred = (centred - low) // 256
    digits.append(centred)
    return np.concatenate(digits, axis=0).astype(jnp.bfloat16)


MESH = pl.DeviceIdType.MESH
LANES = 128
BLOCKS = 64
LENGTH = 2 * BLOCKS
CHUNKS = 5
LINE = 8
PLANE = 64


def stacked_columns(values):
    return np.concatenate([values * 256**digit % modulus for digit in range(3)], axis=1)


def plane_order():
    place = np.arange(BLOCKS)
    core, rest = place // (BLOCKS // 2), place % (BLOCKS // 2)
    return rest * 2 + core


def point_table():
    root = pow(generator, (modulus - 1) // POINTS, modulus)
    exponents = np.arange(POINTS)[:, None] * np.arange(BLOCK)[None, :]
    rows = digit_rows(stacked_columns(powers(root, exponents, POINTS)))
    rows = rows.reshape(3, LINE, PLANE, 3 * BLOCK).transpose(1, 0, 2, 3)
    return rows.reshape(LINE, 3 * PLANE, 3 * BLOCK)


def block_table():
    root = pow(generator, (modulus - 1) // LENGTH, modulus)
    exponents = np.arange(LENGTH)[:, None] * plane_order()[None, :]
    return digit_rows(stacked_columns(powers(root, exponents, LENGTH)))


def block_back_table():
    root = pow(generator, (modulus - 1) // LENGTH, modulus)
    rows = np.concatenate([2 * plane_order() + half for half in range(2)])
    table = powers(root, -rows[:, None] * np.arange(LENGTH)[None, :], LENGTH)
    signed = []
    for sign in (1, -1):
        carry = 1 + sign * powers(root, np.arange(LENGTH), LENGTH)
        signed.append(digit_rows(stacked_columns(table * carry[None, :] % modulus)))
    return np.stack(signed)


def point_back_table():
    root = pow(generator, (modulus - 1) // POINTS, modulus)
    exponents = -np.arange(BLOCK)[:, None] * np.arange(POINTS)[None, :]
    scale = pow(2 * BLOCKS * POINTS, modulus - 2, modulus)
    table = powers(root, exponents, POINTS) * scale % modulus
    return np.stack(
        [digit_rows(stacked_columns(table[:, part : part + BLOCK])) for part in (0, BLOCK)]
    )


def lane_order():
    source = np.arange(LANES).reshape(2, 8, 2, 4).transpose(0, 2, 1, 3).reshape(LANES)
    matrix = np.zeros((LANES, LANES), np.float32)
    matrix[source, np.arange(LANES)] = 1.0
    return matrix.astype(jnp.bfloat16)


def reduced(values):
    quotient = jnp.round(values * inverse_modulus)
    return (values - quotient * modulus_high) - quotient


def folded(low, middle, high):
    return reduced(reduced((reduced(high * 256.0) + middle) * 256.0) + low)


def digits_of(values):
    high = jnp.round(values * (1.0 / 65536.0))
    rest = values - high * 65536.0
    middle = jnp.round(rest * (1.0 / 256.0))
    return [rest - middle * 256.0, middle, high]


def stacked_digits(values):
    return jnp.concatenate([digit.astype(jnp.bfloat16) for digit in digits_of(values)], axis=0)


def matmul(left, right):
    return jnp.dot(left, right, preferred_element_type=jnp.float32)


def thirds(sums):
    rows = sums.shape[0] // 3
    return [sums[part * rows : (part + 1) * rows] for part in range(3)]


def kernel(
    x_ref,
    lane_ref,
    point_ref,
    block_ref,
    back_ref,
    point_back_ref,
    out_ref,
    line_out,
    line_in,
    plane_out,
    plane_in,
    left_hat,
    right_hat,
    product_hat,
    line_send,
    line_recv,
    plane_send,
    plane_recv,
):
    deg = lax.axis_index("deg")
    row = lax.axis_index("row")
    core = lax.rem(deg, 2)
    z_lo = lax.rem(deg // 2, 4)
    y = deg // 8
    x = row // 2
    z_hi = lax.rem(row, 2)
    me_line = x * 2 + core
    me_plane = z_hi * 32 + y * 4 + z_lo

    def line_device(other):
        return (
            (y * 4 + z_lo) * 2 + lax.rem(other, 2),
            (other // 2) * 2 + z_hi,
        )

    def plane_device(other):
        return (
            (lax.rem(other // 4, 8) * 4 + lax.rem(other, 4)) * 2 + core,
            x * 2 + other // 32,
        )

    barrier = pltpu.get_barrier_semaphore()

    @pl.loop(1, LINE)
    def _(step):
        pl.semaphore_signal(
            barrier,
            inc=1,
            device_id=line_device(lax.rem(me_line + step, LINE)),
            device_id_type=MESH,
        )

    @pl.loop(1, PLANE)
    def _(step):
        pl.semaphore_signal(
            barrier,
            inc=1,
            device_id=plane_device(lax.rem(me_plane + step, PLANE)),
            device_id_type=MESH,
        )

    def line_rows(other):
        return pl.ds(pl.multiple_of(other * PLANE, PLANE), PLANE)

    def plane_rows(other):
        return pl.ds(pl.multiple_of(other * LINE, LINE), LINE)

    def line_copy(part, other):
        return pltpu.make_async_remote_copy(
            src_ref=line_out.at[part, line_rows(other)],
            dst_ref=line_in.at[part, line_rows(me_line)],
            send_sem=line_send.at[part],
            recv_sem=line_recv.at[part],
            device_id=line_device(other),
            device_id_type=MESH,
        )

    def plane_copy(part, other):
        return pltpu.make_async_remote_copy(
            src_ref=plane_out.at[part, plane_rows(other)],
            dst_ref=plane_in.at[part, plane_rows(me_plane)],
            send_sem=plane_send.at[part],
            recv_sem=plane_recv.at[part],
            device_id=plane_device(other),
            device_id_type=MESH,
        )

    def wait_line(part, semaphore):
        span = line_in.at[part, pl.ds(0, (LINE - 1) * PLANE)]
        pltpu.make_async_copy(span, span, semaphore.at[part]).wait()

    def wait_plane(part, semaphore):
        span = plane_in.at[part, pl.ds(0, (PLANE - 1) * LINE)]
        pltpu.make_async_copy(span, span, semaphore.at[part]).wait()

    def send_plane(part, make):
        @pl.loop(1, PLANE)
        def _(step):
            other = lax.rem(me_plane + step * PLANE_STRIDE, PLANE)
            if make is not None:
                plane_out[part, plane_rows(other)] = make(other)
            plane_copy(part, other).start()

        own = plane_out[part, plane_rows(me_plane)] if make is None else make(me_plane)
        plane_in[part, plane_rows(me_plane)] = own

    def send_line(part, make):
        @pl.loop(1, LINE)
        def _(step):
            other = lax.rem(me_line + step, LINE)
            if make is not None:
                line_out[part, line_rows(other)] = make(other)
            line_copy(part, other).start()

        own = line_out[part, line_rows(me_line)] if make is None else make(me_line)
        line_in[part, line_rows(me_line)] = own

    def line_to_plane(part):
        send_plane(part, lambda other: line_in[part, pl.ds(other, LINE, stride=PLANE), :])

    def plane_to_line(part):
        send_line(part, lambda other: plane_in[part, pl.ds(other, PLANE, stride=LINE), :])

    def points_of(part):
        stacked = stacked_digits(x_ref[part])
        if part == 0:
            stacked = matmul(stacked, lane_ref[...]).astype(jnp.bfloat16)

        def make(other):
            return folded(*thirds(matmul(point_ref[other], stacked)))

        return make

    first = points_of(0)

    @pl.loop(0, LINE)
    def _(other):
        plane_out[0, pl.ds(other, PLANE, stride=LINE), :] = first(other)

    pl.semaphore_wait(barrier, LINE + PLANE - 2)
    send_plane(0, None)
    for part in range(1, CHUNKS):
        send_line(part, points_of(part))
        if part >= 2:
            wait_line(part - 1, line_recv)
            line_to_plane(part - 1)
    wait_plane(0, plane_recv)
    plane_to_line(0)
    wait_line(CHUNKS - 1, line_recv)
    line_to_plane(CHUNKS - 1)

    def blocks_of(part, group):
        x_of, z_of = group // 2, lax.rem(group, 2)
        pieces = []
        for core_of in range(2):
            line = x_of * 2 + core_of
            if part == 0:
                start = pl.multiple_of(line * PLANE + z_of * 32, 32)
                pieces.append(line_in[part, pl.ds(start, 32), :])
            else:
                start = z_of * 32 * LINE + line
                pieces.append(plane_in[part, pl.ds(start, 32, stride=LINE), :])
        return jnp.concatenate(pieces, axis=0)

    def transform_blocks(part, store):
        @pl.loop(0, LINE // 2)
        def _(pair):
            wide = jnp.concatenate(
                [blocks_of(part, pair * 2), blocks_of(part, pair * 2 + 1)], axis=1
            )
            spectrum = folded(*thirds(matmul(block_ref[...], stacked_digits(wide))))
            store(pair * 2, spectrum[:, :LANES])
            store(pair * 2 + 1, spectrum[:, LANES:])

    def store_left(group, values):
        left_hat[pl.ds(group, LENGTH, stride=8), :] = values

    wait_line(0, line_recv)
    transform_blocks(0, store_left)
    for part in range(1, CHUNKS):

        def store_right(group, values):
            right_hat[pl.ds(group * 4 + (part - 1), LENGTH, stride=32), :] = values

        wait_plane(part, plane_recv)
        transform_blocks(part, store_right)

    batch = 8
    lane = lax.broadcasted_iota(jnp.int32, (8 * batch, LANES), 1)
    window = lane // 32
    low_half = lax.broadcasted_iota(jnp.int32, (8, LANES), 1) < 64

    @pl.loop(0, LENGTH // batch)
    def _(step):
        base = pl.multiple_of(step * 8 * batch, 8 * batch)
        left = left_hat[pl.ds(base, 8 * batch), :]
        factors = []
        for choice in range(4):
            spread = jnp.where(window == choice, left, 0.0)
            spread = spread + pltpu.roll(spread, 64, 1)
            spread = spread + pltpu.roll(spread, 32, 1)
            once = reduced(spread * 256.0)
            twice = reduced(once * 256.0)
            spread = jnp.where(window == 0, spread, jnp.where(window == 1, once, twice))
            factors.append(digits_of(jnp.where(window == 3, 0.0, spread)))
        for index in range(batch):
            rows = slice(8 * index, 8 * index + 8)
            stacked_left = jnp.concatenate(
                [digit[rows] for factor in factors for digit in factor], axis=0
            ).astype(jnp.bfloat16)
            start = pl.multiple_of((step * batch + index) * 32, 32)
            right = digits_of(right_hat[pl.ds(start, 32), :])
            stacked_right = jnp.concatenate(right + [right[2]], axis=0).astype(jnp.bfloat16)
            sums = matmul(stacked_left, stacked_right)
            parts = [
                [sums[24 * choice + 8 * digit : 24 * choice + 8 * digit + 8] for digit in range(3)]
                for choice in range(4)
            ]
            totals = [
                jnp.where(
                    low_half,
                    parts[0][digit] + pltpu.roll(parts[1][digit], 64, 1),
                    pltpu.roll(parts[2][digit], 64, 1) + parts[3][digit],
                )
                for digit in range(3)
            ]
            start = pl.multiple_of(base + 8 * index, 8)
            product_hat[pl.ds(start, 8), :] = folded(*totals)

    first_part, second_part = CHUNKS, CHUNKS + 1
    parity = lax.rem(z_lo, 2)

    @pl.loop(0, LINE // 2)
    def _(pair):
        wide = jnp.concatenate(
            [product_hat[pl.ds(pair * 2 + side, LENGTH, stride=8), :] for side in range(2)], axis=1
        )
        values = folded(*thirds(matmul(back_ref[parity], stacked_digits(wide))))
        for side in range(2):
            group = pair * 2 + side
            x_of, z_of = group // 2, lax.rem(group, 2)
            for core_of in range(2):
                line = x_of * 2 + core_of
                piece = values[32 * core_of : 32 * core_of + 32, LANES * side : LANES * side + LANES]
                plane_out[first_part, pl.ds(z_of * 32 * LINE + line, 32, stride=LINE), :] = piece
                piece = values[
                    64 + 32 * core_of : 96 + 32 * core_of, LANES * side : LANES * side + LANES
                ]
                start = pl.multiple_of(line * PLANE + z_of * 32, 32)
                line_out[second_part, pl.ds(start, 32), :] = piece

    send_line(second_part, None)
    send_plane(first_part, None)
    wait_line(second_part, line_recv)
    line_to_plane(second_part)
    wait_plane(first_part, plane_recv)
    plane_to_line(first_part)

    def coefficients(half, load):
        total = None
        for side in range(2):
            values = jnp.concatenate([load(side * 4 + line) for line in range(4)], axis=0)
            sums = folded(*thirds(matmul(point_back_ref[side], stacked_digits(values))))
            total = sums if total is None else reduced(total + sums)
        out_ref[half] = jnp.where(total < 0.0, total + float(modulus), total)

    wait_line(first_part, line_recv)
    coefficients(0, lambda line: line_in[first_part, pl.ds(line * PLANE, PLANE), :])
    wait_plane(second_part, plane_recv)
    coefficients(1, lambda line: plane_in[second_part, pl.ds(line, PLANE, stride=LINE), :])

    for part in range(CHUNKS + 2):
        wait_line(part, line_send)
        wait_plane(part, plane_send)


PLANE_STRIDE = 1


def shards(left_factor, right_factor):
    local, rows, depth = left_factor.shape
    left = left_factor.reshape(1, local, rows * depth)
    right = right_factor.reshape(local, 2, 4, CD).transpose(2, 0, 1, 3).reshape(4, local, 2 * CD)
    columns = jnp.concatenate([left, right], axis=0)
    parts = CHUNKS + 2
    whole = pl.BlockSpec(memory_space=pltpu.VMEM)
    buffer = pltpu.VMEM((parts, POINTS, LANES), jnp.float32)
    semaphores = pltpu.SemaphoreType.DMA((parts,))
    coeffs = pl.pallas_call(
        kernel,
        out_shape=jax.ShapeDtypeStruct((2, BLOCK, LANES), jnp.float32),
        in_specs=[whole] * 6,
        out_specs=whole,
        scratch_shapes=[buffer] * 4
        + [
            pltpu.VMEM((LENGTH * 8, LANES), jnp.float32),
            pltpu.VMEM((LENGTH * 32, LANES), jnp.float32),
            pltpu.VMEM((LENGTH * 8, LANES), jnp.float32),
        ]
        + [semaphores] * 4,
        compiler_params=pltpu.CompilerParams(
            collective_id=0, has_side_effects=True, vmem_limit_bytes=56 * 2**20
        ),
    )(
        columns,
        jnp.asarray(lane_order()),
        jnp.asarray(point_table()),
        jnp.asarray(block_table()),
        jnp.asarray(block_back_table()),
        jnp.asarray(point_back_table()),
    )
    return (coeffs / modulus).reshape(2 * local, rows, CD)


def solution(mesh):
    placed = P("deg", "row", None)
    return jax.shard_map(
        shards, mesh=mesh, in_specs=(placed, placed), out_specs=placed, check_vma=False
    )
```

profile of v0, /device:TPU:1, one launch (start us, length us, event | category | flops | bytes accessed | tf_op | source)
XLA Modules:
  0.0 94.5 jit_solution(9276120435120841649)
XLA Ops:
  0.0 1.0 %copy.15 = f32[1,256,128]{2,1,0:T(8,128)S(1)} copy(f32[1,256,128]{1,2,0:T(8,128)} %bitcast.9) | data formatting | bytes 262144 | tf_op jit(solution)/shard_map/reshape | solution.py:410
  1.0 1.1 %copy.14 = f32[4,256,2,64]{1,3,2,0:T(8,128)S(1)} copy(f32[4,256,2,64]{1,3,0,2:T(8,128)} %bitcast.8) | data formatting | bytes 1048576 | tf_op jit(solution)/shard_map/transpose | solution.py:411
  2.1 0.2 copy.16
  2.3 0.9 pad_maximum_fusion.x_ref
  3.2 89.3 %shard_map.73 = f32[2,256,128]{2,1,0:T(8,128)} custom-call(f32[5,256,128]{2,1,0:T(8,128)} %pad_maximum_fusion.x_ref, bf16[128,128]{1,0:T(8,128)(2,1)} %constant.13.clone.lane_ref, bf16[8,192,768]{2,1,0:T(8,128)(2,1)} %constant.14.clone.point_ref, bf16[384,192]{1,0:T(8,128)(2,1)} %constant.15.clone.block_ref, bf16[2,384,384]{2,1,0:T(8,128)(2,1)} %constant.16.clone.back_ref, ...), custom_call_target="tpu_custom_call" | custom-call | tf_op jit(solution)/shard_map/pallas_call | solution.py:417
  92.5 1.0 %broadcast_multiply_fusion = f32[2,256,128]{2,1,0:T(8,128)S(1)} fusion(f32[2,256,128]{2,1,0:T(8,128)} %shard_map.73), kind=kLoop, calls=%fused_computation.1 | loop fusion | flops 65536 | bytes 524288 | tf_op jit(solution)/shard_map/div | solution.py:440
  93.4 0.1 copy.17
  93.6 0.9 reshape.15
where the time goes:
time: 94.7 us; the launch traced here: 94.5 us
  Pallas kernels  89.3 us (94%)
  local copies, waits for them, and re-layouts  3.34 us (4%)
  other arithmetic  1.86 us (2%)
    pallas_call x1, Pallas kernels, shards(): pl.pallas_call(kernel, out_shape=jax.ShapeDtypeStruct((2, BLOCK, LANES),...  89.3 us

commit v1 on v0

v1 whole, which is shorter than its diff:
```python
import numpy as np
import jax
import jax.numpy as jnp
from jax import lax
from jax.experimental import pallas as pl
from jax.experimental.pallas import tpu as pltpu
from jax.sharding import PartitionSpec as P

modulus = 7340033
generator = 3
inverse_modulus = 1.0 / modulus
modulus_high = float(modulus - 1)

BLOCK = 256
POINTS = 2 * BLOCK
KD = 64
CD = 64


def powers(root, exponents, order):
    table = np.ones(order, np.int64)
    for position in range(1, order):
        table[position] = table[position - 1] * root % modulus
    return table[exponents % order]


def digit_rows(values):
    centred = np.where(values > modulus // 2, values - modulus, values)
    digits = []
    for _ in range(2):
        low = (centred + 128) % 256 - 128
        digits.append(low)
        centred = (centred - low) // 256
    digits.append(centred)
    return np.concatenate(digits, axis=0).astype(jnp.bfloat16)


MESH = pl.DeviceIdType.MESH
LANES = 128
BLOCKS = 64
LENGTH = 2 * BLOCKS
CHUNKS = 5
LINE = 8
PLANE = 64


def stacked_columns(values):
    return np.concatenate([values * 256**digit % modulus for digit in range(3)], axis=1)


def block_order():
    place = np.arange(BLOCKS)
    return place % LINE * LINE + place // LINE


def point_table():
    root = pow(generator, (modulus - 1) // POINTS, modulus)
    exponents = np.arange(POINTS)[:, None] * np.arange(BLOCK)[None, :]
    rows = digit_rows(stacked_columns(powers(root, exponents, POINTS)))
    rows = rows.reshape(3, LINE, PLANE, 3 * BLOCK).transpose(1, 0, 2, 3)
    return rows.reshape(LINE, 3 * PLANE, 3 * BLOCK)


def block_table():
    root = pow(generator, (modulus - 1) // LENGTH, modulus)
    exponents = np.arange(LENGTH)[:, None] * block_order()[None, :]
    return digit_rows(stacked_columns(powers(root, exponents, LENGTH)))


def block_back_table():
    root = pow(generator, (modulus - 1) // LENGTH, modulus)
    rows = np.concatenate([2 * block_order(), 2 * np.arange(BLOCKS) + 1])
    table = powers(root, -rows[:, None] * np.arange(LENGTH)[None, :], LENGTH)
    signed = []
    for sign in (1, -1):
        carry = 1 + sign * powers(root, np.arange(LENGTH), LENGTH)
        signed.append(digit_rows(stacked_columns(table * carry[None, :] % modulus)))
    return np.stack(signed)


def point_back_table():
    root = pow(generator, (modulus - 1) // POINTS, modulus)
    exponents = -np.arange(BLOCK)[:, None] * np.arange(POINTS)[None, :]
    scale = pow(2 * BLOCKS * POINTS, modulus - 2, modulus)
    table = powers(root, exponents, POINTS) * scale % modulus
    return np.stack(
        [digit_rows(stacked_columns(table[:, part : part + BLOCK])) for part in (0, BLOCK)]
    )


def row_order():
    source = np.arange(LANES).reshape(2, 8, 4, 2).transpose(0, 3, 1, 2).reshape(LANES)
    matrix = np.zeros((LANES, LANES), np.float32)
    matrix[np.arange(LANES), source] = 1.0
    return matrix.astype(jnp.bfloat16)


def reduced(values):
    quotient = jnp.round(values * inverse_modulus)
    return (values - quotient * modulus_high) - quotient


def folded(low, middle, high):
    return reduced(reduced((reduced(high * 256.0) + middle) * 256.0) + low)


def digits_of(values):
    high = jnp.round(values * (1.0 / 65536.0))
    rest = values - high * 65536.0
    middle = jnp.round(rest * (1.0 / 256.0))
    return [rest - middle * 256.0, middle, high]


def stacked_digits(values, axis=0):
    return jnp.concatenate([digit.astype(jnp.bfloat16) for digit in digits_of(values)], axis=axis)


def matmul(left, right):
    return jnp.dot(left, right, preferred_element_type=jnp.float32)


def matmul_transposed(left, right):
    return lax.dot_general(
        left, right, (((1,), (1,)), ((), ())), preferred_element_type=jnp.float32
    )


def thirds(sums):
    rows = sums.shape[0] // 3
    return [sums[part * rows : (part + 1) * rows] for part in range(3)]


def kernel(
    left_ref,
    right_ref,
    order_ref,
    point_ref,
    block_hbm,
    back_hbm,
    point_back_hbm,
    out_ref,
    block_ref,
    back_ref,
    point_back_ref,
    line_out,
    line_in,
    plane_out,
    plane_in,
    left_hat,
    left_digits,
    right_hat,
    product_hat,
    table_sem,
    line_send,
    line_recv,
    plane_send,
    plane_recv,
):
    deg = lax.axis_index("deg")
    row = lax.axis_index("row")
    rest = lax.rem(deg, 8)
    me_line = deg // 8
    me_plane = row * 8 + rest

    def line_device(other):
        return (other * 8 + rest, row)

    def plane_device(other):
        return (me_line * 8 + lax.rem(other, 8), other // 8)

    barrier = pltpu.get_barrier_semaphore()

    @pl.loop(1, LINE)
    def _(step):
        pl.semaphore_signal(
            barrier,
            inc=1,
            device_id=line_device(lax.rem(me_line + step, LINE)),
            device_id_type=MESH,
        )

    @pl.loop(1, PLANE)
    def _(step):
        pl.semaphore_signal(
            barrier,
            inc=1,
            device_id=plane_device(lax.rem(me_plane + step, PLANE)),
            device_id_type=MESH,
        )

    tables = [
        pltpu.make_async_copy(source, target, table_sem.at[index])
        for index, (source, target) in enumerate(
            [(block_hbm, block_ref), (back_hbm, back_ref), (point_back_hbm, point_back_ref)]
        )
    ]
    for table in tables:
        table.start()

    def line_rows(other):
        return pl.ds(pl.multiple_of(other * PLANE, PLANE), PLANE)

    def plane_rows(other):
        return pl.ds(pl.multiple_of(other * LINE, LINE), LINE)

    def line_copy(part, other):
        return pltpu.make_async_remote_copy(
            src_ref=line_out.at[part, line_rows(other)],
            dst_ref=line_in.at[part, line_rows(me_line)],
            send_sem=line_send.at[part],
            recv_sem=line_recv.at[part],
            device_id=line_device(other),
            device_id_type=MESH,
        )

    def plane_copy(part, other):
        return pltpu.make_async_remote_copy(
            src_ref=plane_out.at[part, plane_rows(other)],
            dst_ref=plane_in.at[part, plane_rows(me_plane)],
            send_sem=plane_send.at[part],
            recv_sem=plane_recv.at[part],
            device_id=plane_device(other),
            device_id_type=MESH,
        )

    def wait_line(part, semaphore):
        span = line_in.at[part, pl.ds(0, (LINE - 1) * PLANE)]
        pltpu.make_async_copy(span, span, semaphore.at[part]).wait()

    def wait_plane(part, semaphore):
        span = plane_in.at[part, pl.ds(0, (PLANE - 1) * LINE)]
        pltpu.make_async_copy(span, span, semaphore.at[part]).wait()

    def far_first(step):
        half = step // 2
        odd = lax.rem(step, 2)
        return odd * (3 - half) + (1 - odd) * (4 + half)

    def plane_partner(step):
        outer = step // 8
        pair = outer // 2
        odd = lax.rem(pair, 2)
        shift = odd * (1 - pair // 2) + (1 - odd) * (2 + pair // 2)
        x_other = lax.rem(row // 2 + shift, 4)
        z_here = lax.rem(row, 2) * 4 + rest // 2
        z_other = lax.rem(z_here + far_first(lax.rem(step, 8)), 8)
        core_other = lax.rem(rest + 1 - lax.rem(outer, 2), 2)
        row_other = x_other * 2 + z_other // 4
        return row_other * 8 + lax.rem(z_other, 4) * 2 + core_other

    def send_plane(part, make):
        @pl.loop(0, PLANE - 1, unroll=PLANE_UNROLL)
        def _(step):
            other = plane_partner(step)
            if make is not None:
                plane_out[part, plane_rows(other)] = make(other)
            plane_copy(part, other).start()

        own = plane_out[part, plane_rows(me_plane)] if make is None else make(me_plane)
        plane_in[part, plane_rows(me_plane)] = own

    def send_line(part, make):
        @pl.loop(0, LINE - 1, unroll=LINE - 1)
        def _(step):
            other = lax.rem(me_line + far_first(step), LINE)
            if make is not None:
                line_out[part, line_rows(other)] = make(other)
            line_copy(part, other).start()

        own = line_out[part, line_rows(me_line)] if make is None else make(me_line)
        line_in[part, line_rows(me_line)] = own

    def line_to_plane(part):
        send_plane(part, lambda other: line_in[part, pl.ds(other, LINE, stride=PLANE), :])

    def plane_to_line(part):
        send_line(part, lambda other: plane_in[part, pl.ds(other, PLANE, stride=LINE), :])

    def right_digits(first, count):
        return stacked_digits(right_ref[pl.ds((first - 1) * LANES, count * LANES), :], axis=1)

    def points_of(other, stacked):
        return folded(*thirds(matmul_transposed(point_ref[other], stacked)))

    left = stacked_digits(left_ref[...], axis=1)
    left = matmul(order_ref[...], left).astype(jnp.bfloat16)
    stacked = jnp.concatenate([left, right_digits(1, 1)], axis=0)

    @pl.loop(0, LINE, unroll=POINT_UNROLL)
    def _(other):
        values = points_of(other, stacked)
        plane_out[0, pl.ds(other, PLANE, stride=LINE), :] = values[:, :LANES]
        line_out[1, line_rows(other), :] = values[:, LANES:]

    pl.semaphore_wait(barrier, LINE + PLANE - 2)
    send_line(1, None)
    send_plane(0, None)

    stacked_more = right_digits(2, 2)

    @pl.loop(0, LINE, unroll=POINT_UNROLL)
    def _(other):
        values = points_of(other, stacked_more)
        plane_out[2, pl.ds(other, PLANE, stride=LINE), :] = values[:, :LANES]
        line_out[3, line_rows(other), :] = values[:, LANES:]

    send_line(3, None)
    wait_line(1, line_recv)
    line_to_plane(1)

    stacked_last = right_digits(4, 1)

    @pl.loop(0, LINE, unroll=POINT_UNROLL)
    def _(other):
        line_out[4, line_rows(other), :] = points_of(other, stacked_last)

    wait_plane(0, plane_recv)
    plane_to_line(0)
    send_line(4, None)
    send_plane(2, None)
    wait_line(3, line_recv)
    line_to_plane(3)

    def blocks_of(part, group):
        if part in (0, 2):
            return jnp.concatenate(
                [
                    line_in[part, pl.ds(group * LINE + index, LINE, stride=PLANE), :]
                    for index in range(LINE)
                ],
                axis=0,
            )
        return plane_in[part, pl.ds(pl.multiple_of(group * PLANE, PLANE), PLANE), :]

    def transform_blocks(part):
        @pl.loop(0, LINE // 2, unroll=BLOCK_UNROLL)
        def _(pair):
            wide = jnp.concatenate(
                [blocks_of(part, pair * 2), blocks_of(part, pair * 2 + 1)], axis=1
            )
            spectrum = folded(*thirds(matmul(block_ref[...], stacked_digits(wide))))
            for side in range(2):
                group = pair * 2 + side
                values = spectrum[:, LANES * side : LANES * side + LANES]
                if part == 0:
                    left_hat[pl.ds(group, LENGTH, stride=8), :] = values
                else:
                    right_hat[pl.ds(group * 4 + part - 1, LENGTH, stride=32), :] = values

    batch = 8
    lane = lax.broadcasted_iota(jnp.int32, (8 * batch, LANES), 1)
    window = lane // 32
    low_half = lax.broadcasted_iota(jnp.int32, (8, LANES), 1) < 64

    def prepare_left():
        @pl.loop(0, LENGTH // batch, unroll=LEFT_UNROLL)
        def _(step):
            base = pl.multiple_of(step * 8 * batch, 8 * batch)
            left = left_hat[pl.ds(base, 8 * batch), :]
            factors = []
            for choice in range(4):
                spread = jnp.where(window == choice, left, 0.0)
                for shift in (64, 32):
                    spread = spread + pltpu.roll(spread, shift, 1)
                once = reduced(spread * 256.0)
                twice = reduced(once * 256.0)
                spread = jnp.where(window == 0, spread, jnp.where(window == 1, once, twice))
                factors.append(digits_of(jnp.where(window < 3, spread, 0.0)))
            for index in range(batch):
                rows = slice(8 * index, 8 * index + 8)
                start = pl.multiple_of((step * batch + index) * 96, 96)
                left_digits[pl.ds(start, 96), :] = jnp.concatenate(
                    [digit[rows] for factor in factors for digit in factor], axis=0
                ).astype(jnp.bfloat16)

    def multiply():
        @pl.loop(0, LENGTH // batch, unroll=PRODUCT_UNROLL)
        def _(step):
            for index in range(batch):
                place = step * batch + index
                left = left_digits[pl.ds(pl.multiple_of(place * 96, 96), 96), :]
                right = digits_of(right_hat[pl.ds(pl.multiple_of(place * 32, 32), 32), :])
                right = jnp.concatenate(right + [right[2]], axis=0).astype(jnp.bfloat16)
                sums = matmul(left, right)
                parts = [sums[8 * part : 8 * part + 8] for part in range(12)]
                totals = [
                    jnp.where(low_half, parts[digit], parts[9 + digit])
                    + pltpu.roll(jnp.where(low_half, parts[6 + digit], parts[3 + digit]), 64, 1)
                    for digit in range(3)
                ]
                product_hat[pl.ds(pl.multiple_of(place * 8, 8), 8), :] = folded(*totals)

    tables[0].wait()
    wait_plane(1, plane_recv)
    transform_blocks(1)
    wait_line(0, line_recv)
    transform_blocks(0)
    wait_plane(2, plane_recv)
    plane_to_line(2)
    wait_line(4, line_recv)
    line_to_plane(4)
    prepare_left()
    wait_plane(3, plane_recv)
    transform_blocks(3)
    wait_line(2, line_recv)
    transform_blocks(2)
    wait_plane(4, plane_recv)
    transform_blocks(4)
    multiply()

    first_part, second_part = CHUNKS, CHUNKS + 1
    parity = lax.rem(rest, 2)
    tables[1].wait()

    @pl.loop(0, LINE // 2, unroll=BLOCK_UNROLL)
    def _(pair):
        wide = jnp.concatenate(
            [product_hat[pl.ds(pair * 2 + side, LENGTH, stride=8), :] for side in range(2)], axis=1
        )
        values = folded(*thirds(matmul(back_ref[parity], stacked_digits(wide))))
        for side in range(2):
            group = pair * 2 + side
            mine = values[:, LANES * side : LANES * side + LANES]
            plane_out[first_part, pl.ds(pl.multiple_of(group * PLANE, PLANE), PLANE), :] = mine[:PLANE]
            for line in range(LINE):
                start = pl.multiple_of(line * PLANE + group * LINE, LINE)
                line_out[second_part, pl.ds(start, LINE), :] = mine[
                    PLANE + LINE * line : PLANE + LINE * line + LINE
                ]

    send_line(second_part, None)
    send_plane(first_part, None)
    wait_line(second_part, line_recv)
    line_to_plane(second_part)
    wait_plane(first_part, plane_recv)
    plane_to_line(first_part)

    def coefficients(half, load):
        total = None
        for side in range(2):
            values = jnp.concatenate([load(side * 4 + line) for line in range(4)], axis=0)
            sums = folded(*thirds(matmul(point_back_ref[side], stacked_digits(values))))
            total = sums if total is None else reduced(total + sums)
        total = jnp.where(total < 0.0, total + float(modulus), total)
        out_ref[:, half * BLOCK : half * BLOCK + BLOCK] = (total / float(modulus)).T

    tables[2].wait()
    wait_line(first_part, line_recv)
    coefficients(0, lambda line: line_in[first_part, pl.ds(line * PLANE, PLANE), :])
    wait_plane(second_part, plane_recv)
    coefficients(1, lambda line: plane_in[second_part, pl.ds(line, PLANE, stride=LINE), :])

    for part in range(CHUNKS + 2):
        wait_line(part, line_send)
        wait_plane(part, plane_send)


PLANE_UNROLL = 7
POINT_UNROLL = 2
BLOCK_UNROLL = 2
LEFT_UNROLL = 2
PRODUCT_UNROLL = 4


def shards(left_factor, right_factor):
    local, rows, depth = left_factor.shape
    left = left_factor.transpose(1, 2, 0).reshape(LANES, local)
    right = right_factor.transpose(1, 2, 0).reshape((CHUNKS - 1) * LANES, local)
    parts = CHUNKS + 2
    whole = pl.BlockSpec(memory_space=pltpu.VMEM)
    remote = pl.BlockSpec(memory_space=pl.ANY)
    buffer = pltpu.VMEM((parts, POINTS, LANES), jnp.float32)
    semaphores = pltpu.SemaphoreType.DMA((parts,))
    block, back, point_back = block_table(), block_back_table(), point_back_table()
    coeffs = pl.pallas_call(
        kernel,
        out_shape=jax.ShapeDtypeStruct((LANES, POINTS), jnp.float32),
        in_specs=[whole] * 4 + [remote] * 3,
        out_specs=whole,
        scratch_shapes=[
            pltpu.VMEM(table.shape, jnp.bfloat16) for table in (block, back, point_back)
        ]
        + [buffer] * 4
        + [
            pltpu.VMEM((LENGTH * 8, LANES), jnp.float32),
            pltpu.VMEM((LENGTH * 96, LANES), jnp.bfloat16),
            pltpu.VMEM((LENGTH * 32, LANES), jnp.float32),
            pltpu.VMEM((LENGTH * 8, LANES), jnp.float32),
        ]
        + [pltpu.SemaphoreType.DMA((3,))]
        + [semaphores] * 4,
        compiler_params=pltpu.CompilerParams(
            collective_id=0, has_side_effects=True, vmem_limit_bytes=56 * 2**20
        ),
    )(
        left,
        right,
        jnp.asarray(row_order()),
        jnp.asarray(point_table()),
        jnp.asarray(block),
        jnp.asarray(back),
        jnp.asarray(point_back),
    )
    return coeffs.reshape(rows, CD, 2 * local).transpose(2, 0, 1)


def solution(mesh):
    placed = P("deg", "row", None)
    return jax.shard_map(
        shards, mesh=mesh, in_specs=(placed, placed), out_specs=placed, check_vma=False
    )
```

time: 94.7 us -> 78.7 us (0.83)
  the two profiles are of different devices: /device:TPU:1 before, /device:TPU:2 now
where the time goes in v1:
time: 78.7 us; the launch traced here: 78.6 us
  Pallas kernels  76.9 us (98%)
  local copies, waits for them, and re-layouts  1.67 us (2%)
    pallas_call x1, Pallas kernels, shards(): pl.pallas_call(kernel, out_shape=jax.ShapeDtypeStruct((LANES, POINTS), jn...  76.9 us
    unnamed x1, local copies, waits for them, and re-layouts  1.67 us

profile of v1, /device:TPU:2, one launch (start us, length us, event | category | flops | bytes accessed | tf_op | source)
XLA Modules:
  0.0 78.6 jit_solution(3165532908111994053)
XLA Ops:
  0.0 76.9 %shard_map.73 = f32[128,512]{1,0:T(8,128)} custom-call(f32[128,256]{1,0:T(8,128)} %bitcast.11, f32[512,256]{1,0:T(8,128)} %bitcast.10, bf16[128,128]{1,0:T(8,128)(2,1)} %constant.10.clone.order_ref, bf16[8,192,768]{2,1,0:T(8,128)(2,1)} %constant.11.clone.point_ref, bf16[384,192]{1,0:T(8,128)(2,1)} %constant.12.clone.block_hbm, ...), custom_call_target="tpu_custom_call" | custom-call | tf_op jit(solution)/shard_map/pallas_call | solution.py:475
  76.9 1.7 %copy.9 = f32[512,2,64]{0,2,1:T(8,128)} copy(f32[512,2,64]{0,2,1:T(8,128)} %bitcast.9) | data formatting | bytes 524288

commit v2 on v1

--- a/solution.py
+++ b/solution.py
@@ -49,8 +49,7 @@
 
 
 def block_order():
-    place = np.arange(BLOCKS)
-    return place % LINE * LINE + place // LINE
+    return np.arange(BLOCKS).reshape(8, 4, 2).transpose(2, 1, 0).reshape(BLOCKS)
 
 
 def point_table():
@@ -69,7 +68,7 @@
 
 def block_back_table():
     root = pow(generator, (modulus - 1) // LENGTH, modulus)
-    rows = np.concatenate([2 * block_order(), 2 * np.arange(BLOCKS) + 1])
+    rows = np.concatenate([2 * block_order(), 2 * block_order() + 1])
     table = powers(root, -rows[:, None] * np.arange(LENGTH)[None, :], LENGTH)
     signed = []
     for sign in (1, -1):
@@ -134,11 +133,12 @@
     left_ref,
     right_ref,
     order_ref,
-    point_ref,
+    point_hbm,
     block_hbm,
     back_hbm,
     point_back_hbm,
     out_ref,
+    point_ref,
     block_ref,
     back_ref,
     point_back_ref,
@@ -150,6 +150,7 @@
     left_digits,
     right_hat,
     product_hat,
+    point_sem,
     table_sem,
     line_send,
     line_recv,
@@ -160,17 +161,26 @@
     row = lax.axis_index("row")
     rest = lax.rem(deg, 8)
     me_line = deg // 8
-    me_plane = row * 8 + rest
+    core = lax.rem(rest, 2)
+    z_lo = rest // 2
+    me_plane = core * 32 + row * 4 + z_lo
+
+    def point_copy(other):
+        return pltpu.make_async_copy(point_hbm.at[other], point_ref.at[other], point_sem.at[other])
+
+    for other in range(LINE):
+        point_copy(other).start()
 
     def line_device(other):
         return (other * 8 + rest, row)
 
     def plane_device(other):
-        return (me_line * 8 + lax.rem(other, 8), other // 8)
+        device = me_line * 8 + lax.rem(other, 4) * 2 + other // 32
+        return (device, lax.rem(other // 4, 8))
 
     barrier = pltpu.get_barrier_semaphore()
 
-    @pl.loop(1, LINE)
+    @pl.loop(1, LINE, unroll=LINE - 1)
     def _(step):
         pl.semaphore_signal(
             barrier,
@@ -179,7 +189,7 @@
             device_id_type=MESH,
         )
 
-    @pl.loop(1, PLANE)
+    @pl.loop(1, PLANE, unroll=PLANE_UNROLL)
     def _(step):
         pl.semaphore_signal(
             barrier,
@@ -236,17 +246,19 @@
         odd = lax.rem(step, 2)
         return odd * (3 - half) + (1 - odd) * (4 + half)
 
-    def plane_partner(step):
-        outer = step // 8
-        pair = outer // 2
+    def core_partner(step, core_other):
+        pair = step // 8
         odd = lax.rem(pair, 2)
         shift = odd * (1 - pair // 2) + (1 - odd) * (2 + pair // 2)
         x_other = lax.rem(row // 2 + shift, 4)
-        z_here = lax.rem(row, 2) * 4 + rest // 2
+        z_here = lax.rem(row, 2) * 4 + z_lo
         z_other = lax.rem(z_here + far_first(lax.rem(step, 8)), 8)
-        core_other = lax.rem(rest + 1 - lax.rem(outer, 2), 2)
-        row_other = x_other * 2 + z_other // 4
-        return row_other * 8 + lax.rem(z_other, 4) * 2 + core_other
+        return core_other * 32 + (x_other * 2 + z_other // 4) * 4 + lax.rem(z_other, 4)
+
+    def plane_partner(step):
+        outer = step // 8
+        core_other = lax.rem(core + 1 - lax.rem(outer, 2), 2)
+        return core_partner(outer // 2 * 8 + lax.rem(step, 8), core_other)
 
     def send_plane(part, make):
         @pl.loop(0, PLANE - 1, unroll=PLANE_UNROLL)
@@ -288,6 +300,7 @@
 
     @pl.loop(0, LINE, unroll=POINT_UNROLL)
     def _(other):
+        point_copy(other).wait()
         values = points_of(other, stacked)
         plane_out[0, pl.ds(other, PLANE, stride=LINE), :] = values[:, :LANES]
         line_out[1, line_rows(other), :] = values[:, LANES:]
@@ -305,8 +318,7 @@
         line_out[3, line_rows(other), :] = values[:, LANES:]
 
     send_line(3, None)
-    wait_line(1, line_recv)
-    line_to_plane(1)
+    send_plane(2, None)
 
     stacked_last = right_digits(4, 1)
 
@@ -314,23 +326,34 @@
     def _(other):
         line_out[4, line_rows(other), :] = points_of(other, stacked_last)
 
+    send_line(4, None)
+    wait_line(1, line_recv)
+    line_to_plane(1)
     wait_plane(0, plane_recv)
     plane_to_line(0)
-    send_line(4, None)
-    send_plane(2, None)
     wait_line(3, line_recv)
     line_to_plane(3)
+    wait_plane(2, plane_recv)
+    plane_to_line(2)
+    wait_line(4, line_recv)
+    line_to_plane(4)
 
     def blocks_of(part, group):
         if part in (0, 2):
             return jnp.concatenate(
                 [
-                    line_in[part, pl.ds(group * LINE + index, LINE, stride=PLANE), :]
+                    line_in[part, pl.ds(group * 4 + index // 4 * 32 + index % 4, 8, stride=64), :]
                     for index in range(LINE)
                 ],
                 axis=0,
             )
-        return plane_in[part, pl.ds(pl.multiple_of(group * PLANE, PLANE), PLANE), :]
+        return jnp.concatenate(
+            [
+                plane_in[part, pl.ds(pl.multiple_of(side * 256 + group * 32, 32), 32), :]
+                for side in range(2)
+            ],
+            axis=0,
+        )
 
     def transform_blocks(part):
         @pl.loop(0, LINE // 2, unroll=BLOCK_UNROLL)
@@ -395,21 +418,16 @@
     transform_blocks(1)
     wait_line(0, line_recv)
     transform_blocks(0)
-    wait_plane(2, plane_recv)
-    plane_to_line(2)
-    wait_line(4, line_recv)
-    line_to_plane(4)
     prepare_left()
     wait_plane(3, plane_recv)
     transform_blocks(3)
+    wait_plane(4, plane_recv)
+    transform_blocks(4)
     wait_line(2, line_recv)
     transform_blocks(2)
-    wait_plane(4, plane_recv)
-    transform_blocks(4)
     multiply()
 
-    first_part, second_part = CHUNKS, CHUNKS + 1
-    parity = lax.rem(rest, 2)
+    parity = lax.rem(z_lo, 2)
     tables[1].wait()
 
     @pl.loop(0, LINE // 2, unroll=BLOCK_UNROLL)
@@ -421,41 +439,133 @@
         for side in range(2):
             group = pair * 2 + side
             mine = values[:, LANES * side : LANES * side + LANES]
-            plane_out[first_part, pl.ds(pl.multiple_of(group * PLANE, PLANE), PLANE), :] = mine[:PLANE]
+            for half in range(2):
+                part = CHUNKS + half
+                first = PLANE * half
+                plane_out[part, pl.ds(pl.multiple_of(group * 32, 32), 32), :] = mine[
+                    first : first + 32
+                ]
+                for z_of in range(4):
+                    line_out[part, pl.ds(32 + group * 4 + z_of, 8, stride=64), :] = mine[
+                        first + 32 + 8 * z_of : first + 40 + 8 * z_of
+                    ]
+
+    def half_rows(other):
+        return pl.ds(pl.multiple_of(other * PLANE + 32, 32), 32)
+
+    def half_copy(part, other):
+        return pltpu.make_async_remote_copy(
+            src_ref=line_out.at[part, half_rows(other)],
+            dst_ref=line_in.at[part, half_rows(me_line)],
+            send_sem=line_send.at[part],
+            recv_sem=line_recv.at[part],
+            device_id=line_device(other),
+            device_id_type=MESH,
+        )
+
+    def send_half_line(part):
+        @pl.loop(0, LINE - 1, unroll=LINE - 1)
+        def _(step):
+            half_copy(part, lax.rem(me_line + far_first(step), LINE)).start()
+
+        line_in[part, half_rows(me_line), :] = line_out[part, half_rows(me_line), :]
+
+    def wait_half_line(part, semaphore):
+        span = line_in.at[part, pl.ds(0, (LINE - 1) * 32)]
+        pltpu.make_async_copy(span, span, semaphore.at[part]).wait()
+
+    def send_core(part, core_other, make):
+        def put(other):
+            if make is not None:
+                plane_out[part, plane_rows(other)] = make(other)
+
+        @pl.loop(0, 31, unroll=CORE_UNROLL)
+        def _(step):
+            other = core_partner(step, core_other)
+            put(other)
+            plane_copy(part, other).start()
+
+        last = core_partner(31, core_other)
+        put(last)
+
+        @pl.when(core != core_other)
+        def _():
+            plane_copy(part, last).start()
+
+        @pl.when(core == core_other)
+        def _():
+            plane_in[part, plane_rows(me_plane)] = plane_out[part, plane_rows(me_plane)]
+
+    def wait_core_sent(part, core_other):
+        @pl.when(core != core_other)
+        def _():
+            span = plane_in.at[part, pl.ds(0, 32 * LINE)]
+            pltpu.make_async_copy(span, span, plane_send.at[part]).wait()
+
+        @pl.when(core == core_other)
+        def _():
+            span = plane_in.at[part, pl.ds(0, 31 * LINE)]
+            pltpu.make_async_copy(span, span, plane_send.at[part]).wait()
+
+    for half in range(2):
+        send_half_line(CHUNKS + half)
+        send_core(CHUNKS + half, 0, None)
+    for half in range(2):
+        part, last = CHUNKS + half, CHUNKS + 2 + half
+
+        @pl.when(core == 0)
+        def _():
+            wait_plane(part, plane_recv)
+            send_line(
+                last, lambda other: plane_in[part, pl.ds(other, PLANE, stride=LINE), :]
+            )
+
+        wait_half_line(part, line_recv)
+        send_core(last, 1, lambda other: line_in[part, pl.ds(other, LINE, stride=PLANE), :])
+
+    def coefficients(half):
+        part = CHUNKS + 2 + half
+
+        @pl.when(core == 0)
+        def _():
+            wait_line(part, line_recv)
+
+        @pl.when(core == 1)
+        def _():
+            wait_plane(part, plane_recv)
             for line in range(LINE):
-                start = pl.multiple_of(line * PLANE + group * LINE, LINE)
-                line_out[second_part, pl.ds(start, LINE), :] = mine[
-                    PLANE + LINE * line : PLANE + LINE * line + LINE
+                line_in[part, line_rows(line), :] = plane_in[
+                    part, pl.ds(line, PLANE, stride=LINE), :
                 ]
 
-    send_line(second_part, None)
-    send_plane(first_part, None)
-    wait_line(second_part, line_recv)
-    line_to_plane(second_part)
-    wait_plane(first_part, plane_recv)
-    plane_to_line(first_part)
-
-    def coefficients(half, load):
         total = None
         for side in range(2):
-            values = jnp.concatenate([load(side * 4 + line) for line in range(4)], axis=0)
+            values = line_in[part, pl.ds(side * BLOCK, BLOCK), :]
             sums = folded(*thirds(matmul(point_back_ref[side], stacked_digits(values))))
             total = sums if total is None else reduced(total + sums)
         total = jnp.where(total < 0.0, total + float(modulus), total)
         out_ref[:, half * BLOCK : half * BLOCK + BLOCK] = (total / float(modulus)).T
 
     tables[2].wait()
-    wait_line(first_part, line_recv)
-    coefficients(0, lambda line: line_in[first_part, pl.ds(line * PLANE, PLANE), :])
-    wait_plane(second_part, plane_recv)
-    coefficients(1, lambda line: plane_in[second_part, pl.ds(line, PLANE, stride=LINE), :])
-
-    for part in range(CHUNKS + 2):
+    coefficients(0)
+    coefficients(1)
+
+    for part in range(CHUNKS):
         wait_line(part, line_send)
         wait_plane(part, plane_send)
+    for half in range(2):
+        wait_half_line(CHUNKS + half, line_send)
+        wait_core_sent(CHUNKS + half, 0)
+        wait_core_sent(CHUNKS + 2 + half, 1)
+
+    @pl.when(core == 0)
+    def _():
+        for half in range(2):
+            wait_line(CHUNKS + 2 + half, line_send)
 
 
 PLANE_UNROLL = 7
+CORE_UNROLL = 31
 POINT_UNROLL = 2
 BLOCK_UNROLL = 2
 LEFT_UNROLL = 2
@@ -466,19 +576,20 @@
     local, rows, depth = left_factor.shape
     left = left_factor.transpose(1, 2, 0).reshape(LANES, local)
     right = right_factor.transpose(1, 2, 0).reshape((CHUNKS - 1) * LANES, local)
-    parts = CHUNKS + 2
+    parts = CHUNKS + 4
     whole = pl.BlockSpec(memory_space=pltpu.VMEM)
     remote = pl.BlockSpec(memory_space=pl.ANY)
     buffer = pltpu.VMEM((parts, POINTS, LANES), jnp.float32)
     semaphores = pltpu.SemaphoreType.DMA((parts,))
-    block, back, point_back = block_table(), block_back_table(), point_back_table()
+    point, block = point_table(), block_table()
+    back, point_back = block_back_table(), point_back_table()
     coeffs = pl.pallas_call(
         kernel,
         out_shape=jax.ShapeDtypeStruct((LANES, POINTS), jnp.float32),
-        in_specs=[whole] * 4 + [remote] * 3,
+        in_specs=[whole] * 3 + [remote] * 4,
         out_specs=whole,
         scratch_shapes=[
-            pltpu.VMEM(table.shape, jnp.bfloat16) for table in (block, back, point_back)
+            pltpu.VMEM(table.shape, jnp.bfloat16) for table in (point, block, back, point_back)
         ]
         + [buffer] * 4
         + [
@@ -487,7 +598,7 @@
             pltpu.VMEM((LENGTH * 32, LANES), jnp.float32),
             pltpu.VMEM((LENGTH * 8, LANES), jnp.float32),
         ]
-        + [pltpu.SemaphoreType.DMA((3,))]
+        + [pltpu.SemaphoreType.DMA((LINE,)), pltpu.SemaphoreType.DMA((3,))]
         + [semaphores] * 4,
         compiler_params=pltpu.CompilerParams(
             collective_id=0, has_side_effects=True, vmem_limit_bytes=56 * 2**20
@@ -496,7 +607,7 @@
         left,
         right,
         jnp.asarray(row_order()),
-        jnp.asarray(point_table()),
+        jnp.asarray(point),
         jnp.asarray(block),
         jnp.asarray(back),
         jnp.asarray(point_back),

time: 78.7 us -> 73.9 us (0.939)
  the two profiles are of different devices: /device:TPU:2 before, /device:TPU:1 now
where the time goes in v2:
time: 73.9 us; the launch traced here: 73.7 us
  Pallas kernels  72.1 us (98%)
  local copies, waits for them, and re-layouts  1.67 us (2%)
    pallas_call x1, Pallas kernels, shards(): pl.pallas_call(kernel, out_shape=jax.ShapeDtypeStruct((LANES, POINTS), jn...  72.1 us
    unnamed x1, local copies, waits for them, and re-layouts  1.67 us

profile of v2, /device:TPU:1, one launch (start us, length us, event | category | flops | bytes accessed | tf_op | source)
XLA Modules:
  0.0 73.7 jit_solution(10464571922958303597)
XLA Ops:
  0.0 72.1 %shard_map.73 = f32[128,512]{1,0:T(8,128)} custom-call(f32[128,256]{1,0:T(8,128)} %bitcast.11, f32[512,256]{1,0:T(8,128)} %bitcast.10, bf16[128,128]{1,0:T(8,128)(2,1)} %constant.10.clone.order_ref, bf16[8,192,768]{2,1,0:T(8,128)(2,1)} %constant.11.clone.point_hbm, bf16[384,192]{1,0:T(8,128)(2,1)} %constant.12.clone.block_hbm, ...), custom_call_target="tpu_custom_call" | custom-call | tf_op jit(solution)/shard_map/pallas_call | solution.py:586
  72.1 1.7 %copy.9 = f32[512,2,64]{0,2,1:T(8,128)} copy(f32[512,2,64]{0,2,1:T(8,128)} %bitcast.9) | data formatting | bytes 524288

commit v3 on v2

--- a/solution.py
+++ b/solution.py
@@ -68,12 +68,13 @@
 
 def block_back_table():
     root = pow(generator, (modulus - 1) // LENGTH, modulus)
-    rows = np.concatenate([2 * block_order(), 2 * block_order() + 1])
-    table = powers(root, -rows[:, None] * np.arange(LENGTH)[None, :], LENGTH)
     signed = []
     for sign in (1, -1):
         carry = 1 + sign * powers(root, np.arange(LENGTH), LENGTH)
-        signed.append(digit_rows(stacked_columns(table * carry[None, :] % modulus)))
+        for half in range(2):
+            rows = 2 * block_order() + half
+            table = powers(root, -rows[:, None] * np.arange(LENGTH)[None, :], LENGTH)
+            signed.append(digit_rows(stacked_columns(table * carry[None, :] % modulus)))
     return np.stack(signed)
 
 
@@ -430,24 +431,23 @@
     parity = lax.rem(z_lo, 2)
     tables[1].wait()
 
-    @pl.loop(0, LINE // 2, unroll=BLOCK_UNROLL)
-    def _(pair):
-        wide = jnp.concatenate(
-            [product_hat[pl.ds(pair * 2 + side, LENGTH, stride=8), :] for side in range(2)], axis=1
-        )
-        values = folded(*thirds(matmul(back_ref[parity], stacked_digits(wide))))
-        for side in range(2):
-            group = pair * 2 + side
-            mine = values[:, LANES * side : LANES * side + LANES]
-            for half in range(2):
-                part = CHUNKS + half
-                first = PLANE * half
-                plane_out[part, pl.ds(pl.multiple_of(group * 32, 32), 32), :] = mine[
-                    first : first + 32
-                ]
+    def leave_blocks(half):
+        part = CHUNKS + half
+
+        @pl.loop(0, LINE // 2, unroll=BLOCK_UNROLL)
+        def _(pair):
+            wide = jnp.concatenate(
+                [product_hat[pl.ds(pair * 2 + side, LENGTH, stride=8), :] for side in range(2)],
+                axis=1,
+            )
+            values = folded(*thirds(matmul(back_ref[parity * 2 + half], stacked_digits(wide))))
+            for side in range(2):
+                group = pair * 2 + side
+                mine = values[:, LANES * side : LANES * side + LANES]
+                plane_out[part, pl.ds(pl.multiple_of(group * 32, 32), 32), :] = mine[:32]
                 for z_of in range(4):
                     line_out[part, pl.ds(32 + group * 4 + z_of, 8, stride=64), :] = mine[
-                        first + 32 + 8 * z_of : first + 40 + 8 * z_of
+                        32 + 8 * z_of : 40 + 8 * z_of
                     ]
 
     def half_rows(other):
@@ -508,6 +508,7 @@
             pltpu.make_async_copy(span, span, plane_send.at[part]).wait()
 
     for half in range(2):
+        leave_blocks(half)
         send_half_line(CHUNKS + half)
         send_core(CHUNKS + half, 0, None)
     for half in range(2):
@@ -566,10 +567,10 @@
 
 PLANE_UNROLL = 7
 CORE_UNROLL = 31
-POINT_UNROLL = 2
-BLOCK_UNROLL = 2
+POINT_UNROLL = 4
+BLOCK_UNROLL = 4
 LEFT_UNROLL = 2
-PRODUCT_UNROLL = 4
+PRODUCT_UNROLL = 8
 
 
 def shards(left_factor, right_factor):
@@ -585,7 +586,7 @@
     back, point_back = block_back_table(), point_back_table()
     coeffs = pl.pallas_call(
         kernel,
-        out_shape=jax.ShapeDtypeStruct((LANES, POINTS), jnp.float32),
+        out_shape=pltpu.VMEM((LANES, POINTS), jnp.float32),
         in_specs=[whole] * 3 + [remote] * 4,
         out_specs=whole,
         scratch_shapes=[

time: 73.9 us -> 70.4 us (0.953)
  Pallas kernels: 72.1 us -> 69.6 us
  local copies, waits for them, and re-layouts: 1.67 us -> 0.71 us
    pallas_call x1, Pallas kernels: 72.1 us -> 69.6 us  [shards(): pl.pallas_call(kernel, out_shape=pltpu.VMEM((LANES, POINTS), jnp.float32)...]
    unnamed x1, local copies, waits for them, and re-layouts: 1.67 us -> 0.71 us
where the time goes in v3:
time: 70.4 us; the launch traced here: 70.3 us
  Pallas kernels  69.6 us (99%)
  local copies, waits for them, and re-layouts  0.71 us (1%)
    pallas_call x1, Pallas kernels, shards(): pl.pallas_call(kernel, out_shape=pltpu.VMEM((LANES, POINTS), jnp.float32)...  69.6 us

profile of v3, /device:TPU:1, one launch (start us, length us, event | category | flops | bytes accessed | tf_op | source)
XLA Modules:
  0.0 70.3 jit_solution(13606415674838038366)
XLA Ops:
  0.0 69.6 %shard_map.73 = f32[128,512]{1,0:T(8,128)S(1)} custom-call(f32[128,256]{1,0:T(8,128)} %bitcast.11, f32[512,256]{1,0:T(8,128)} %bitcast.10, bf16[128,128]{1,0:T(8,128)(2,1)} %constant.10.clone.order_ref, bf16[8,192,768]{2,1,0:T(8,128)(2,1)} %constant.11.clone.point_hbm, bf16[384,192]{1,0:T(8,128)(2,1)} %constant.12.clone.block_hbm, ...), custom_call_target="tpu_custom_call" | custom-call | tf_op jit(solution)/shard_map/pallas_call | solution.py:587
  69.6 0.7 %copy.9 = f32[512,2,64]{0,2,1:T(8,128)} copy(f32[512,2,64]{0,2,1:T(8,128)S(1)} %bitcast.9) | data formatting | bytes 524288

commit v4 on v3

--- a/solution.py
+++ b/solution.py
@@ -299,15 +299,21 @@
     left = matmul(order_ref[...], left).astype(jnp.bfloat16)
     stacked = jnp.concatenate([left, right_digits(1, 1)], axis=0)
 
+    pl.semaphore_wait(barrier, LINE + PLANE - 2)
+
     @pl.loop(0, LINE, unroll=POINT_UNROLL)
-    def _(other):
+    def _(step):
+        other = lax.rem(me_line + 1 + step, LINE)
         point_copy(other).wait()
         values = points_of(other, stacked)
         plane_out[0, pl.ds(other, PLANE, stride=LINE), :] = values[:, :LANES]
         line_out[1, line_rows(other), :] = values[:, LANES:]
 
-    pl.semaphore_wait(barrier, LINE + PLANE - 2)
-    send_line(1, None)
+        @pl.when(step < LINE - 1)
+        def _():
+            line_copy(1, other).start()
+
+    line_in[1, line_rows(me_line), :] = line_out[1, line_rows(me_line), :]
     send_plane(0, None)
 
     stacked_more = right_digits(2, 2)

time: 70.4 us -> 73.8 us (1.048)
  Pallas kernels: 69.6 us -> 73 us
    pallas_call x1, Pallas kernels: 69.6 us -> 73 us  [shards(): pl.pallas_call(kernel, out_shape=pltpu.VMEM((LANES, POINTS), jnp.float32)...]
where the time goes in v4:
time: 73.8 us; the launch traced here: 73.7 us
  Pallas kernels  73 us (99%)
    pallas_call x1, Pallas kernels, shards(): pl.pallas_call(kernel, out_shape=pltpu.VMEM((LANES, POINTS), jnp.float32)...  73 us

profile of v4, /device:TPU:1, one launch (start us, length us, event | category | flops | bytes accessed | tf_op | source)
XLA Modules:
  0.0 73.7 jit_solution(13063374829345689291)
XLA Ops:
  0.0 73.0 %shard_map.73 = f32[128,512]{1,0:T(8,128)S(1)} custom-call(f32[128,256]{1,0:T(8,128)} %bitcast.11, f32[512,256]{1,0:T(8,128)} %bitcast.10, bf16[128,128]{1,0:T(8,128)(2,1)} %constant.10.clone.order_ref, bf16[8,192,768]{2,1,0:T(8,128)(2,1)} %constant.11.clone.point_hbm, bf16[384,192]{1,0:T(8,128)(2,1)} %constant.12.clone.block_hbm, ...), custom_call_target="tpu_custom_call" | custom-call | tf_op jit(solution)/shard_map/pallas_call | solution.py:593
  73.0 0.7 copy.9
